TPU v7x, 32 devices: a whole 2x2x4 slice. The times are simulated.
32 devices in a mesh: dp: 4 (over z), feature: 4 (over y, x), view: 2 (over core).
Axes of the slice: x: 2, y: 2, z: 4, core: 2. Of those that a mesh axis runs over, the one named last changes fastest.
Arguments:
- views: bfloat16 [2, 1024, 8192], P('view', 'dp'), may hold values from -64 to 64
- weight: bfloat16 [8192, 4096], P(None, ('feature', 'view')), may hold values from -1 to 1
Outputs:
- proj_grad: bfloat16 [2, 1024, 4096], P(None, 'dp', ('feature', 'view'))
- loss_value: float32 [], replicated
All inputs are finite; a program needn't handle non-finite values.
Results may differ from a plain program's by a relative error of at most 0.0034.
Values may be sent and summed in bfloat16 or wider, within the bound.
A program may use at most 64 MiB of HBM per device.

v0:
```python
import jax
import jax.numpy as jnp
from jax import lax
from jax.sharding import PartitionSpec as P

eps = 1e-05
redundancy_weight = 0.0051


def from_partner(block, axis, bit):
    count = lax.axis_size(axis)
    route = []
    for low in range(count):
        high = low | 1 << bit
        if high != low and high < count:
            route += [(low, high), (high, low)]
    return lax.ppermute(block, axis, route)


def local(views, weight):
    batch = views.shape[1] * lax.axis_size("dp")
    local_cols = weight.shape[1]
    total_cols = local_cols * lax.axis_size("feature") * lax.axis_size("view")
    col_block = lax.axis_index("feature") * lax.axis_size("view") + lax.axis_index("view")
    partner = from_partner(views, "view", 0)
    view_side = lax.axis_index("view")
    first_view = jnp.where(view_side == 0, views[0], partner[0])
    second_view = jnp.where(view_side == 0, partner[0], views[0])
    projected = jnp.stack(
        [
            jnp.dot(first_view, weight, preferred_element_type=jnp.float32),
            jnp.dot(second_view, weight, preferred_element_type=jnp.float32),
        ]
    )
    col_mean = lax.psum(jnp.sum(projected, axis=1, keepdims=True), "dp") / batch
    centered = projected - col_mean
    col_var = lax.psum(jnp.sum(centered * centered, axis=1, keepdims=True), "dp") / batch
    inv_std = lax.rsqrt(col_var + eps)
    standard = centered * inv_std
    rounded = standard.astype(jnp.bfloat16)
    second_all = lax.all_gather(rounded[1], ("feature", "view"), axis=1, tiled=True)
    contract_rows = (((0,), (0,)), ((), ()))
    sliced = rounded[0]
    corr_block = (
        lax.psum_scatter(
            lax.dot_general(sliced, second_all, contract_rows, preferred_element_type=jnp.float32),
            "dp",
            scatter_dimension=0,
            tiled=True,
        )
        / batch
    )
    own_rows = corr_block.shape[0]
    first_idx = (
        col_block * local_cols
        + lax.axis_index("dp") * own_rows
        + lax.broadcasted_iota(jnp.int32, corr_block.shape, 0)
    )
    second_idx = lax.broadcasted_iota(jnp.int32, corr_block.shape, 1)
    on_diag = first_idx == second_idx
    loss_part = jnp.sum(
        jnp.where(on_diag, (1.0 - corr_block) ** 2, redundancy_weight * corr_block * corr_block)
    )
    loss_value = lax.psum(loss_part, ("dp", "feature", "view")) / total_cols
    grad_block = jnp.where(
        on_diag, -2.0 * (1.0 - corr_block), 2.0 * redundancy_weight * corr_block
    ).astype(jnp.bfloat16)
    grad_full = lax.all_gather(grad_block, "dp", axis=0, tiled=True)
    grad_first = lax.dot_general(
        second_all, grad_full, (((1,), (1,)), ((), ())), preferred_element_type=jnp.float32
    )
    sliced = grad_full
    grad_second = lax.psum_scatter(
        lax.dot_general(
            sliced, rounded[0], (((0,), (1,)), ((), ())), preferred_element_type=jnp.float32
        ),
        ("feature", "view"),
        scatter_dimension=0,
        tiled=True,
    ).T
    grad_std = jnp.stack([grad_first, grad_second])
    sum_grad, sum_cross = lax.psum(
        (
            jnp.sum(grad_std, axis=1, keepdims=True),
            jnp.sum(grad_std * standard, axis=1, keepdims=True),
        ),
        "dp",
    )
    proj_grad = (inv_std * (grad_std - sum_grad / batch - standard * (sum_cross / batch))).astype(
        jnp.bfloat16
    )
    return (proj_grad, loss_value)


def solution(mesh):
    placed = (P("view", "dp", None), P(None, ("feature", "view")))
    return jax.shard_map(
        local,
        mesh=mesh,
        in_specs=placed,
        out_specs=(P(None, "dp", ("feature", "view")), P()),
        check_vma=False,
    )
```

profile of v0, /device:TPU:0, one launch (start us, length us, event | category | flops | bytes accessed | tf_op | source)
XLA Modules:
  0.0 390.1 jit_solution(4943483751446568161)
XLA Ops:
  7.2 0.5 collective-permute-start
  7.7 7.1 %collective-permute-done = bf16[1,256,8192]{2,1,0:T(8,128)(2,1)} collective-permute-done((bf16[1,256,8192]{2,1,0:T(8,128)(2,1)}, bf16[1,256,8192]{2,1,0:T(8,128)(2,1)}, u32[]{:S(2)}, u32[]{:S(2)}) %collective-permute-start) | collective-permute-done | bytes 4194336 | tf_op jit(solution)/shard_map/ppermute | solution.py:17
  14.9 7.0 %fusion.18 = f32[1,256,512]{2,1,0:T(8,128)S(1)} fusion(bf16[8192,512]{1,0:T(8,128)(2,1)} %param.3, bf16[1,256,8192]{2,1,0:T(8,128)(2,1)} %collective-permute-done, bf16[1,256,8192]{2,1,0:T(8,128)(2,1)} %param.2, pred[]{:T(512)S(6)} %eq.7), kind=kOutput, calls=%fused_computation.17 | convolution fusion | flops 2149580800 | bytes 17301504 | tf_op jit(solution)/shard_map/dot_general | solution.py:32
  21.9 2.3 fusion.15
  24.2 0.1 fusion.23
  24.3 13.3 %psum.35 = f32[2,1,512]{2,0,1:T(2,128)S(1)} all-reduce(f32[2,1,512]{2,0,1:T(2,128)S(1)} %bitcast.50), channel_id=1, replica_groups=mesh['dp'=4,'feature'=4,'view'=2] {'dp'}, use_global_device_ids=true, to_apply=%region_1.2 | all-reduce | flops 1024 | bytes 8192 | tf_op jit(solution)/shard_map/psum | solution.py:35
  37.6 0.1 multiply_reduce_fusion.1
  37.8 8.4 %psum.36 = f32[2,1,512]{2,0,1:T(2,128)S(1)} all-reduce(f32[2,1,512]{2,0,1:T(2,128)S(1)} %bitcast.51), channel_id=1, replica_groups=mesh['dp'=4,'feature'=4,'view'=2] {'dp'}, use_global_device_ids=true, to_apply=%region_3.4 | all-reduce | flops 1024 | bytes 8192 | tf_op jit(solution)/shard_map/psum | solution.py:37
  46.1 0.1 fusion.21
  46.3 0.7 slice.9
  47.0 0.0 reduce-scatter.3.cloned.1.call-start
  47.1 28.0 %all-gather.6.cloned.1.call-done = bf16[1,256,4096]{2,1,0:T(8,128)(2,1)} async-done(((bf16[1,256,512]{2,1,0:T(8,128)(2,1)}), bf16[1,256,4096]{2,1,0:T(8,128)(2,1)}) %all-gather.6.cloned.1.call-update) | async-done | bytes 2097168 | tf_op jit(solution)/shard_map/all_gather | solution.py:41
  75.0 6.1 %fusion.10 = f32[512,4096]{1,0:T(8,128)} fusion(bf16[1,256,4096]{2,1,0:T(8,128)(2,1)} %all-gather.6.cloned.1.call-done, bf16[2,256,512]{2,1,0:T(8,128)(2,1)S(1)} %fusion.21), kind=kOutput, calls=%fused_computation.10 | convolution fusion | flops 1073741824 | bytes 10747904 | tf_op jit(solution)/shard_map/dot_general | solution.py:46
  81.2 0.0 all-gather.4.cloned.1.call-start
  81.2 144.6 %reduce-scatter.3.cloned.1.call-done = f32[128,4096]{1,0:T(8,128)} async-done(((f32[512,4096]{1,0:T(8,128)}), f32[128,4096]{1,0:T(8,128)}) %reduce-scatter.3.cloned.1.call-update) | async-done | bytes 2097168 | tf_op jit(solution)/shard_map/reduce_scatter | solution.py:45
  225.8 4.1 %select_reduce_fusion = (f32[]{:T(128)}, bf16[128,4096]{1,0:T(8,128)(2,1)}) fusion(f32[128,4096]{1,0:T(8,128)} %reduce-scatter.3.cloned.1.call-done, s32[128]{0:T(128)S(1)} %iota_add_fusion), kind=kLoop, calls=%fused_computation.12 | loop fusion | flops 6291455 | bytes 3146244 | tf_op jit(solution)/shard_map/reduce_sum | solution.py:61
  229.9 81.6 %all-gather.4.cloned.1.call-done = bf16[512,4096]{1,0:T(8,128)(2,1)} async-done(((bf16[128,4096]{1,0:T(8,128)(2,1)}), bf16[512,4096]{1,0:T(8,128)(2,1)}) %all-gather.4.cloned.1.call-update) | async-done | bytes 4194320 | tf_op jit(solution)/shard_map/all_gather | solution.py:68
  311.5 5.4 %fusion.24 = f32[4096,256]{0,1:T(8,128)} fusion(bf16[512,4096]{1,0:T(8,128)(2,1)} %all-gather.4.cloned.1.call-done, bf16[2,256,512]{2,1,0:T(8,128)(2,1)S(1)} %fusion.21), kind=kOutput, calls=%fused_computation.28 | convolution fusion | flops 1073741824 | bytes 8650752 | tf_op jit(solution)/shard_map/dot_general | solution.py:74
  316.9 39.2 %psum.39 = f32[]{:T(128)} all-reduce(f32[]{:T(128)} %get-tuple-element.6), channel_id=1, replica_groups=mesh['dp'=4,'feature'=4,'view'=2] {'dp','feature','view'}, use_global_device_ids=true, to_apply=%region_11.12 | all-reduce | flops 1 | bytes 8 | tf_op jit(solution)/shard_map/psum | solution.py:64
  356.8 4.5 %fusion.12 = f32[1,256,512]{2,1,0:T(8,128)S(1)} fusion(bf16[512,4096]{1,0:T(8,128)(2,1)} %all-gather.4.cloned.1.call-done, bf16[1,256,4096]{2,1,0:T(8,128)(2,1)} %all-gather.6.cloned.1.call-done), kind=kOutput, calls=%fused_computation.15 | convolution fusion | flops 1073741824 | bytes 6815744 | tf_op jit(solution)/shard_map/dot_general | solution.py:69
  361.2 5.9 %reduce-scatter.5.cloned.1.call-done = f32[512,256]{0,1:T(8,128)} async-done(((f32[4096,256]{0,1:T(8,128)}), f32[512,256]{0,1:T(8,128)}) %reduce-scatter.5.cloned.1.call-update) | async-done | bytes 524304 | tf_op jit(solution)/shard_map/reduce_scatter | solution.py:73
  367.1 1.3 fusion.22
  368.4 11.9 %all-reduce = (f32[2,1,512]{2,0,1:T(2,128)S(1)}, f32[2,1,512]{2,0,1:T(2,128)S(1)}) all-reduce(f32[2,1,512]{2,0,1:T(2,128)S(1)} %bitcast.49, f32[2,1,512]{2,0,1:T(2,128)S(1)} %bitcast.48), channel_id=1, replica_groups=mesh['dp'=4,'feature'=4,'view'=2] {'dp'}, use_global_device_ids=true, to_apply=%region_9.10 | all-reduce | flops 2048 | bytes 16384 | tf_op jit(solution)/shard_map/psum | solution.py:82
  380.3 2.1 multiply_convert_fusion
  (14 shorter events, 0.2 us)
Async XLA Ops:
  7.2 67.9 %all-gather.6.cloned.1.call-start = ((), (), s32[]{:S(2)}) async-start(), calls=%async_computation.5 | async-start | bytes 2359296 | tf_op jit(solution)/shard_map/all_gather | solution.py:41
  7.2 7.6 %collective-permute-start = (bf16[1,256,8192]{2,1,0:T(8,128)(2,1)}, bf16[1,256,8192]{2,1,0:T(8,128)(2,1)}, u32[]{:S(2)}, u32[]{:S(2)}) collective-permute-start(bf16[1,256,8192]{2,1,0:T(8,128)(2,1)} %param.2), channel_id=1, source_target_pairs={{0,1},{1,0},{2,3},{3,2},{4,5},{5,4},{6,7},{7,6},{8,9},{9,8},{10,11... | collective-permute-start | bytes 12582920 | tf_op jit(solution)/shard_map/ppermute | solution.py:17
  7.7 14.1 %copy-start = (bf16[8192,512]{1,0:T(8,128)(2,1)S(1)}, bf16[8192,512]{1,0:T(8,128)(2,1)}, u32[]{:S(2)}) copy-start(bf16[8192,512]{1,0:T(8,128)(2,1)} %param.3) | copy-start | bytes 25165828
  7.7 14.1 %copy-start.1 = (bf16[1,256,8192]{2,1,0:T(8,128)(2,1)S(1)}, bf16[1,256,8192]{2,1,0:T(8,128)(2,1)}, u32[]{:S(2)}) copy-start(bf16[1,256,8192]{2,1,0:T(8,128)(2,1)} %param.2) | copy-start | bytes 12582916
  47.0 178.8 %reduce-scatter.3.cloned.1.call-start = ((), (), s32[]{:S(2)}) async-start(), calls=%async_computation.2 | async-start | bytes 10485760 | tf_op jit(solution)/shard_map/reduce_scatter | solution.py:45
  81.2 230.3 %all-gather.4.cloned.1.call-start = ((), (), s32[]{:S(2)}) async-start(), calls=%async_computation.3 | async-start | bytes 5242880 | tf_op jit(solution)/shard_map/all_gather | solution.py:68
  229.9 137.3 %reduce-scatter.5.cloned.1.call-start = ((), (), s32[]{:S(2)}) async-start(), calls=%async_computation.4 | async-start | bytes 4718592 | tf_op jit(solution)/shard_map/reduce_scatter | solution.py:73
Sparse Core Ops, SparseCore 0:
  47.2 27.8 all-gather.5
  81.3 144.4 reduce-scatter.2
  230.0 81.4 all-gather.3
  317.1 50.0 reduce-scatter.4
where the time goes:
time: 391 us; the launch traced here: 390 us
  waiting for transfers between devices  267 us (68%)
  blocking collectives  72.8 us (19%)
  matrix products  25.3 us (6%)
  between operations  15.6 us (4%)
  other arithmetic  7.82 us (2%)
    reduce_scatter x1, waiting for transfers between devices, local(): lax.psum_scatter(lax.dot_general(sliced, second_all, contract_rows, prefe...  145 us
    all_gather x1, waiting for transfers between devices, local(): grad_full = lax.all_gather(grad_block, 'dp', axis=0, tiled=True)  81.6 us
    psum x1, blocking collectives, local(): loss_value = lax.psum(loss_part, ('dp', 'feature', 'view')) / total_cols  39.2 us
    all_gather x1, waiting for transfers between devices, local(): lax.all_gather(rounded[1], ('feature', 'view'), axis=1, tiled=True)  28 us
    psum x1, blocking collectives, local(): col_mean = lax.psum(jnp.sum(projected, axis=1, keepdims=True), 'dp') / batch  13.3 us
    psum x1, blocking collectives, local(): lax.psum((jnp.sum(grad_std, axis=1, keepdims=True), jnp.sum(grad_std * st...  11.9 us
    psum x1, blocking collectives, local(): lax.psum(jnp.sum(centered * centered, axis=1, keepdims=True), 'dp') / batch  8.37 us
  transfers between devices with their start and end apart: 5, of which 5 were waited for; matrix products, arithmetic and copies ran while one was open for 1% of the time, Pallas kernels for 0%

commit v1 on v0

v1 whole, which is shorter than its diff:
```python
import jax
import jax.numpy as jnp
from jax import lax
from jax.sharding import PartitionSpec as P

eps = 1e-05
redundancy_weight = 0.0051


def from_partner(block, axis, bit):
    count = lax.axis_size(axis)
    route = []
    for low in range(count):
        high = low | 1 << bit
        if high != low and high < count:
            route += [(low, high), (high, low)]
    return lax.ppermute(block, axis, route)


def plain(views, weight):
    shards = lax.axis_size("dp")
    local_rows = views.shape[1]
    batch = local_rows * shards
    total_cols = weight.shape[1] * lax.axis_size("feature") * lax.axis_size("view")
    partner = from_partner(views, "view", 0)
    first_here = lax.axis_index("view") == 0
    own = jnp.dot(views[0], weight, preferred_element_type=jnp.float32)
    other = jnp.dot(partner[0], weight, preferred_element_type=jnp.float32)
    projected = jnp.stack([jnp.where(first_here, own, other), jnp.where(first_here, other, own)])
    local_mean = jnp.mean(projected, axis=1, keepdims=True)
    spread = projected - local_mean
    local_sq = jnp.sum(spread * spread, axis=1, keepdims=True)
    stats = lax.all_gather(jnp.concatenate([local_mean, local_sq], axis=1), "dp")
    means, squares = stats[:, :, :1], stats[:, :, 1:]
    col_mean = jnp.mean(means, axis=0)
    shift = means - col_mean
    col_var = (jnp.sum(squares, axis=0) + local_rows * jnp.sum(shift * shift, axis=0)) / batch
    inv_std = lax.rsqrt(col_var + eps)
    standard = (projected - col_mean) * inv_std
    rounded = standard.astype(jnp.bfloat16)
    all_rows = lax.all_gather(rounded, "dp", axis=1, tiled=True)
    gram = lax.dot_general(
        rounded, all_rows, (((2,), (2,)), ((0,), (0,))), preferred_element_type=jnp.float32
    )
    gram = lax.psum(gram.astype(jnp.bfloat16), ("feature", "view"))
    diag = (
        jnp.sum(all_rows[0].astype(jnp.float32) * all_rows[1].astype(jnp.float32), axis=0) / batch
    )
    squares_part = jnp.sum(gram[0].astype(jnp.float32) * gram[1].astype(jnp.float32)) / (
        batch * float(batch)
    )
    diag_part = jnp.sum((1.0 - diag) ** 2 - redundancy_weight * diag * diag)
    members = lax.axis_size("feature") * lax.axis_size("view")
    grad_std = lax.dot_general(
        gram[::-1], all_rows, (((2,), (1,)), ((0,), (0,))), preferred_element_type=jnp.float32
    ) * (2.0 * redundancy_weight / batch)
    on_diag = (-2.0 * (1.0 - diag)).astype(jnp.bfloat16).astype(
        jnp.float32
    ) - 2.0 * redundancy_weight * diag
    grad_std = grad_std + rounded[::-1].astype(jnp.float32) * on_diag
    sum_grad, sum_cross = lax.psum(
        (
            jnp.sum(grad_std, axis=1, keepdims=True),
            jnp.sum(grad_std * standard, axis=1, keepdims=True),
        ),
        "dp",
    )
    loss_value = (
        lax.psum(
            redundancy_weight * squares_part / members + diag_part / shards,
            ("dp", "feature", "view"),
        )
        / total_cols
    )
    proj_grad = (inv_std * (grad_std - sum_grad / batch - standard * (sum_cross / batch))).astype(
        jnp.bfloat16
    )
    return (proj_grad, loss_value)


def solution(mesh):
    placed = (P("view", "dp", None), P(None, ("feature", "view")))
    return jax.shard_map(
        plain,
        mesh=mesh,
        in_specs=placed,
        out_specs=(P(None, "dp", ("feature", "view")), P()),
        check_vma=False,
    )
```

time: 391 us -> 213 us (0.54)
  waiting for transfers between devices: 267 us -> 101 us
  blocking collectives: 72.8 us -> 64.6 us
  matrix products: 25.3 us -> 18.5 us
    reduce_scatter x2 -> x0, waiting for transfers between devices: 150 us -> none  [the longest x1 145 us: local(): lax.psum_scatter(lax.dot_general(sliced, second_all, contract_rows, prefe...]
    all_gather x2 -> x1, waiting for transfers between devices: 110 us -> 47.1 us  [plain(): all_rows = lax.all_gather(rounded, 'dp', axis=1, tiled=True)]
    psum x0 -> x1, waiting for transfers between devices: none -> 53.9 us  [plain(): gram = lax.psum(gram.astype(jnp.bfloat16), ('feature', 'view'))]
    psum x4 -> x2, blocking collectives: 72.8 us -> 49.9 us  [the longest x1 39.1 us: plain(): lax.psum(redundancy_weight * squares_part / members + diag_part / shards,...]
    all_gather x0 -> x1, blocking collectives: none -> 14.7 us  [plain(): lax.all_gather(jnp.concatenate([local_mean, local_sq], axis=1), 'dp')]
    ppermute x1, waiting for transfers between devices: 7.12 us -> 0.01 us  [from_partner(): return lax.ppermute(block, axis, route)]
    dot_general x5 -> x4, matrix products: 25.3 us -> 18.5 us  [the longest x1 7.11 us: plain(): own = jnp.dot(views[0], weight, preferred_element_type=jnp.float32)]
    rev x0 -> x2, local copies, waits for them, and re-layouts: none -> 4.15 us  [the longest x1 2.28 us: plain(): gram[::-1]]
  transfers between devices with their start and end apart: 5 -> 3, of which waited for: 5 -> 2; matrix products, arithmetic and copies ran while one was open for 1% -> 4% of each run, Pallas kernels for 0% -> 0%
where the time goes in v1:
time: 213 us
  waiting for transfers between devices  101 us (47%)
  blocking collectives  64.6 us (30%)
  matrix products  18.5 us (9%)
  between operations  17.2 us (8%)
  other arithmetic  6.62 us (3%)
  local copies, waits for them, and re-layouts  4.16 us (2%)
    psum x1, waiting for transfers between devices, plain(): gram = lax.psum(gram.astype(jnp.bfloat16), ('feature', 'view'))  53.9 us
    all_gather x1, waiting for transfers between devices, plain(): all_rows = lax.all_gather(rounded, 'dp', axis=1, tiled=True)  47.1 us
    psum x1, blocking collectives, plain(): lax.psum(redundancy_weight * squares_part / members + diag_part / shards,...  39.1 us
    all_gather x1, blocking collectives, plain(): lax.all_gather(jnp.concatenate([local_mean, local_sq], axis=1), 'dp')  14.7 us
    psum x1, blocking collectives, plain(): lax.psum((jnp.sum(grad_std, axis=1, keepdims=True), jnp.sum(grad_std * st...  10.7 us
    dot_general x1, matrix products, plain(): own = jnp.dot(views[0], weight, preferred_element_type=jnp.float32)  7.11 us
    dot_general x1, matrix products, plain(): other = jnp.dot(partner[0], weight, preferred_element_type=jnp.float32)  4.51 us
  transfers between devices with their start and end apart: 3, of which 2 were waited for; matrix products, arithmetic and copies ran while one was open for 4% of the time, Pallas kernels for 0%

profile of v1, /device:TPU:0, one launch (start us, length us, event | category | flops | bytes accessed | tf_op | source)
XLA Modules:
  0.0 212.6 jit_solution(15508676452602548389)
XLA Ops:
  7.2 0.0 all-gather.3.cloned.1.call-start
  7.2 0.5 collective-permute-start
  7.7 7.1 %fusion.2 = f32[256,512]{1,0:T(8,128)S(1)} fusion(bf16[8192,512]{1,0:T(8,128)(2,1)} %param.3, bf16[1,256,8192]{2,1,0:T(8,128)(2,1)} %param.2), kind=kOutput, calls=%fused_computation.2 | convolution fusion | flops 2147483648 | bytes 13107200 | tf_op jit(solution)/shard_map/dot_general | solution.py:27
  14.9 4.5 %select_bitcast_fusion.1 = (f32[1,256,512]{2,1,0:T(8,128)S(1)}, f32[1,256,512]{2,1,0:T(8,128)S(1)}) fusion(f32[256,512]{1,0:T(8,128)S(1)} %fusion.2, pred[]{:T(512)S(6)} %eq.3, bf16[8192,512]{1,0:T(8,128)(2,1)S(1)} %copy-done.1, bf16[1,256,8192]{2,1,0:T(8,128)(2,1)} %collective-permute-done), kind=kOutput, calls=%fused_computation.16 | convolution fusion | flops 2147745792 | bytes 14155777 | tf_op jit(solution)/shard_map/dot_general | solution.py:28
  19.4 0.1 fusion.6
  19.5 0.1 multiply_reduce_fusion.3
  19.7 14.7 %all-gather = f32[8,2,512]{2,1,0:T(2,128)S(1)} all-gather(f32[2,2,512]{2,1,0:T(2,128)S(1)} %pad_maximum_fusion.1), channel_id=2, replica_groups=mesh['dp'=4,'feature'=4,'view'=2] {'dp'}, dimensions={0}, use_global_device_ids=true | all-gather | bytes 40960 | tf_op jit(solution)/shard_map/all_gather | solution.py:33
  34.4 0.1 multiply_reduce_fusion.4
  34.5 0.9 fusion.5
  35.4 0.0 all-gather.3.cloned.1.call-update
  35.4 0.0 all-reduce.3.cloned.1.call-start
  35.5 47.1 %all-gather.3.cloned.1.call-done = bf16[2,1024,512]{2,1,0:T(8,128)(2,1)} async-done(((bf16[2,256,512]{2,1,0:T(8,128)(2,1)}), bf16[2,1024,512]{2,1,0:T(8,128)(2,1)}) %all-gather.3.cloned.1.call-update) | async-done | bytes 2097168 | tf_op jit(solution)/shard_map/all_gather | solution.py:41
  82.6 3.6 %convolution_convert_fusion = bf16[2,256,1024]{2,1,0:T(8,128)(2,1)} fusion(bf16[2,256,512]{2,1,0:T(8,128)(2,1)} %fusion.5, bf16[2,1024,512]{2,1,0:T(8,128)(2,1)} %all-gather.3.cloned.1.call-done), kind=kOutput, calls=%fused_computation.5 | convolution fusion | flops 537395200 | bytes 3670016 | tf_op jit(solution)/shard_map/dot_general | solution.py:42
  86.2 0.0 all-reduce.3.cloned.1.call-update
  86.2 0.3 multiply_reduce_fusion
  86.6 0.6 subtract_reduce_fusion
  87.8 53.9 %all-reduce.3.cloned.1.call-done = bf16[2,256,1024]{2,1,0:T(8,128)(2,1)} async-done(((bf16[2,256,1024]{2,1,0:T(8,128)(2,1)}), bf16[2,256,1024]{2,1,0:T(8,128)(2,1)}) %all-reduce.3.cloned.1.call-update) | async-done | bytes 1048592 | tf_op jit(solution)/shard_map/psum | solution.py:45
  141.7 2.1 multiply_reduce_fusion.1
  144.4 1.9 rev.7
  146.3 39.1 %psum.31 = f32[]{:T(128)} all-reduce(f32[]{:T(128)S(6)} %add.37), channel_id=1, replica_groups=mesh['dp'=4,'feature'=4,'view'=2] {'dp','feature','view'}, use_global_device_ids=true, to_apply=%region_13.14 | all-reduce | flops 1 | bytes 8 | tf_op jit(solution)/shard_map/psum | solution.py:69
  186.1 2.3 %rev.6 = bf16[2,256,1024]{2,1,0:T(8,128)(2,1)} reverse(bf16[2,256,1024]{2,1,0:T(8,128)(2,1)} %all-reduce.3.cloned.1.call-done), dimensions={0} | reverse | bytes 2097152 | tf_op jit(solution)/shard_map/rev | solution.py:55
  188.4 3.2 %fusion.7 = (f32[2,512]{1,0:T(2,128)S(1)}, f32[2,512]{1,0:T(2,128)S(1)}, f32[2,256,512]{2,1,0:T(8,128)}) fusion(f32[2,512]{1,0:T(2,128)S(1)} %add_rsqrt_fusion, f32[2,512]{1,0:T(2,128)S(1)} %broadcast_multiply_fusion, f32[1,256,512]{2,1,0:T(8,128)S(1)} %get-tuple-element.9, f32[1,256,512]{2,1,0:T(8,128)S(1)} %get-tuple-element.8, ...), kind=kOutput, calls=%fused_computation.30 | convolution fusion | flops 539490304 | bytes 5785600 | tf_op jit(solution)/shard_map/dot_general | solution.py:54
  191.6 10.7 %all-reduce = (f32[2,1,512]{2,0,1:T(2,128)S(1)}, f32[2,1,512]{2,0,1:T(2,128)S(1)}) all-reduce(f32[2,1,512]{2,0,1:T(2,128)S(1)} %bitcast.28, f32[2,1,512]{2,0,1:T(2,128)S(1)} %bitcast.27), channel_id=1, replica_groups=mesh['dp'=4,'feature'=4,'view'=2] {'dp'}, use_global_device_ids=true, to_apply=%region_10.11 | all-reduce | flops 2048 | bytes 16384 | tf_op jit(solution)/shard_map/psum | solution.py:61
  202.4 2.3 %multiply_convert_fusion = bf16[2,256,512]{2,1,0:T(8,128)(2,1)} fusion(f32[2,256,512]{2,1,0:T(8,128)} %get-tuple-element.12, f32[2,512]{1,0:T(2,128)S(1)} %get-tuple-element.13, f32[2,512]{1,0:T(2,128)S(1)} %get-tuple-element.14, f32[2,512]{1,0:T(2,128)S(1)} %broadcast_multiply_fusion, f32[2,512]{1,0:T(2,128)S(1)} %add_rsqrt_fusion, ...), kind=kLoop, calls=%fused_computation.10 | loop fusion | flops 2097152 | bytes 2637824 | tf_op jit(solution)/shard_map/convert_element_type | solution.py:75
  (13 shorter events, 0.1 us)
Async XLA Ops:
  7.2 75.4 %all-gather.3.cloned.1.call-start = ((), (), s32[]{:S(2)}) async-start(), calls=%async_computation | async-start | bytes 2621440 | tf_op jit(solution)/shard_map/all_gather | solution.py:41
  7.2 7.6 %collective-permute-start = (bf16[1,256,8192]{2,1,0:T(8,128)(2,1)}, bf16[1,256,8192]{2,1,0:T(8,128)(2,1)}, u32[]{:S(2)}, u32[]{:S(2)}) collective-permute-start(bf16[1,256,8192]{2,1,0:T(8,128)(2,1)} %param.2), channel_id=1, source_target_pairs={{0,1},{1,0},{2,3},{3,2},{4,5},{5,4},{6,7},{7,6},{8,9},{9,8},{10,11... | collective-permute-start | bytes 12582920 | tf_op jit(solution)/shard_map/ppermute | solution.py:17
  7.7 7.1 %copy-start.1 = (bf16[8192,512]{1,0:T(8,128)(2,1)S(1)}, bf16[8192,512]{1,0:T(8,128)(2,1)}, u32[]{:S(2)}) copy-start(bf16[8192,512]{1,0:T(8,128)(2,1)} %param.3) | copy-start | bytes 25165828
  35.4 106.2 %all-reduce.3.cloned.1.call-start = ((), (), s32[]{:S(2)}) async-start(), calls=%async_computation.1 | async-start | bytes 2097152 | tf_op jit(solution)/shard_map/psum | solution.py:45
  82.6 3.7 %copy-start = (bf16[2,1024,512]{2,1,0:T(8,128)(2,1)S(1)}, bf16[2,1024,512]{2,1,0:T(8,128)(2,1)}, u32[]{:S(2)}) copy-start(bf16[2,1024,512]{2,1,0:T(8,128)(2,1)} %all-gather.3.cloned.1.call-done) | copy-start | bytes 6291460
Sparse Core Ops, SparseCore 0:
  35.6 46.9 all-gather.2
  86.3 55.2 all-reduce.2

commit v2 on v1

--- a/solution.py
+++ b/solution.py
@@ -1,6 +1,10 @@
+import functools
+
 import jax
 import jax.numpy as jnp
 from jax import lax
+from jax.experimental import pallas as pl
+from jax.experimental.pallas import tpu as pltpu
 from jax.sharding import PartitionSpec as P
 
 eps = 1e-05
@@ -78,10 +82,424 @@
     return (proj_grad, loss_value)
 
 
+chunks = 8
+vmem_bytes = 58 * 1024 * 1024
+bf16, f32 = jnp.bfloat16, jnp.float32
+
+
+def head_kernel(
+    n,
+    features,
+    views_ref,
+    w_ref,
+    out_ref,
+    loss_ref,
+    w_all,
+    x_all,
+    proj,
+    acc,
+    inv,
+    rall,
+    k_send,
+    k_recv,
+    k_red,
+    k_full,
+    stat_send,
+    stat_recv,
+    fin_send,
+    fin_recv,
+    dg_send,
+    dg_recv,
+    d_part,
+    sq_acc,
+    w_sem,
+    x_sem,
+    xs_sem,
+    xr_sem,
+    st_s,
+    st_r,
+    z_s,
+    z_r,
+    a_s,
+    a_r,
+    b_s,
+    b_r,
+    f_s,
+    f_r,
+    g_s,
+    g_r,
+):
+    members = 2 * features
+    rows, width = x_all.shape[1:]
+    cols = w_all.shape[1]
+    batch = rows * n
+    step = width // chunks
+    part = rows // members
+    d = lax.axis_index("dp")
+    v = lax.axis_index("view")
+    me = lax.axis_index("feature") * 2 + v
+    u = 1 - v
+
+    def mate(o):
+        t = lax.rem(me + o, members)
+        return t, {"feature": lax.div(t, 2), "view": lax.rem(t, 2)}
+
+    def remote(src, dst, ssem, rsem, where):
+        return pltpu.make_async_remote_copy(
+            src_ref=src,
+            dst_ref=dst,
+            send_sem=ssem,
+            recv_sem=rsem,
+            device_id=where,
+            device_id_type=pl.DeviceIdType.MESH,
+        )
+
+    def drain(ref, sem):
+        pltpu.make_async_copy(ref, ref, sem).wait()
+
+    def span(c):
+        return pl.ds(pl.multiple_of(c * step, step), step)
+
+    def w_copy(c):
+        return pltpu.make_async_copy(w_ref.at[span(c), :], w_all.at[span(c), :], w_sem.at[c])
+
+    def x_copy(c):
+        return pltpu.make_async_copy(
+            views_ref.at[0, :, span(c)], x_all.at[0, :, span(c)], x_sem.at[c]
+        )
+
+    def x_swap(c):
+        return remote(
+            views_ref.at[0, :, span(c)],
+            x_all.at[1, :, span(c)],
+            xs_sem.at[c],
+            xr_sem.at[c],
+            {"view": u},
+        )
+
+    barrier = pltpu.get_barrier_semaphore()
+    for o in range(1, members):
+        pl.semaphore_signal(
+            barrier, inc=1, device_id=mate(o)[1], device_id_type=pl.DeviceIdType.MESH
+        )
+    for o in range(1, n):
+        pl.semaphore_signal(
+            barrier,
+            inc=1,
+            device_id={"dp": lax.rem(d + o, n)},
+            device_id_type=pl.DeviceIdType.MESH,
+        )
+    for c in range(chunks):
+        x_copy(c).start()
+        w_copy(c).start()
+    pl.semaphore_wait(barrier, members - 1 + n - 1)
+    for c in range(chunks):
+        x_swap(c).start()
+
+    def multiply(slot, view, low, high):
+        def body(c, carry):
+            if slot == 0:
+                x_copy(c).wait()
+                w_copy(c).wait()
+            else:
+                x_swap(c).wait_recv()
+            proj[view] += jnp.dot(
+                x_all[slot, :, span(c)], w_all[span(c), :], preferred_element_type=f32
+            )
+            return carry
+
+        lax.fori_loop(low, high, body, 0)
+
+    row_of = lax.broadcasted_iota(jnp.int32, (8, cols), 0)
+
+    def send_stats(view):
+        p = proj[view]
+        mean = jnp.sum(p, axis=0, keepdims=True) / rows
+        spread = p - mean
+        square = jnp.sum(spread * spread, axis=0, keepdims=True)
+        stat_send[view] = jnp.where(row_of == 0, mean, square)
+        for o in range(1, n):
+            remote(
+                stat_send.at[view],
+                stat_recv.at[view, d],
+                st_s.at[view],
+                st_r.at[view],
+                {"dp": lax.rem(d + o, n)},
+            ).start()
+        pltpu.make_async_copy(stat_send.at[view], stat_recv.at[view, d], st_r.at[view]).start()
+
+    def z_copy(b, view, side):
+        return remote(
+            rall.at[b, view],
+            rall.at[b, view],
+            z_s.at[side, b, view],
+            z_r.at[b, view],
+            {"dp": jnp.clip(d + 1 - 2 * side, 0, n - 1)},
+        )
+
+    def pass_on(b, view, side):
+        @pl.when((d < n - 1) if side == 0 else (d > 0))
+        def _():
+            z_copy(b, view, side).start()
+
+    def standardize(view):
+        drain(stat_recv.at[view], st_r.at[view])
+        mean = jnp.zeros((1, cols), f32)
+        for k in range(n):
+            mean += stat_recv[view, k, 0:1]
+        mean = mean / n
+        var = jnp.zeros((1, cols), f32)
+        for k in range(n):
+            shift = stat_recv[view, k, 0:1] - mean
+            var += stat_recv[view, k, 1:2] + rows * (shift * shift)
+        scale = lax.rsqrt(var / batch + eps)
+        inv[view] = jnp.broadcast_to(scale, (8, cols))
+        s = (proj[view] - mean) * scale
+        proj[view] = s
+        rall[d, view] = s.astype(bf16)
+        pass_on(d, view, 0)
+        pass_on(d, view, 1)
+
+    def gram_send(b, view):
+        g = lax.dot_general(
+            rall[d, view], rall[b, view], (((1,), (1,)), ((), ())), preferred_element_type=f32
+        )
+        k_send[b, view] = g.astype(bf16).reshape(members, part, rows)
+        for o in range(1, members):
+            t, where = mate(o)
+            remote(
+                k_send.at[b, view, t],
+                k_recv.at[b, view, me],
+                a_s.at[b, view],
+                a_r.at[b, view],
+                where,
+            ).start()
+        pltpu.make_async_copy(
+            k_send.at[b, view, me], k_recv.at[b, view, me], a_r.at[b, view]
+        ).start()
+
+    def gram_sum(b, view):
+        drain(k_recv.at[b, view], a_r.at[b, view])
+        total = k_recv[b, view, 0].astype(f32)
+        for k in range(1, members):
+            total += k_recv[b, view, k].astype(f32)
+        k_red[b, view] = total.astype(bf16)
+        for o in range(1, members):
+            remote(
+                k_red.at[b, view],
+                k_full.at[b, view, me],
+                b_s.at[b, view],
+                b_r.at[b, view],
+                mate(o)[1],
+            ).start()
+        pltpu.make_async_copy(k_red.at[b, view], k_full.at[b, view, me], b_r.at[b, view]).start()
+
+    def diagonal(b):
+        cross = rall[b, 0].astype(f32) * rall[b, 1].astype(f32)
+        d_part[b] = jnp.broadcast_to(jnp.sum(cross, axis=0, keepdims=True), (8, cols))
+
+    def gram_use(b):
+        for view in range(2):
+            drain(k_full.at[b, view], b_r.at[b, view])
+        first = k_full[b, 0].reshape(rows, rows)
+        second = k_full[b, 1].reshape(rows, rows)
+        acc[0] += jnp.dot(second, rall[b, 0], preferred_element_type=f32)
+        acc[1] += jnp.dot(first, rall[b, 1], preferred_element_type=f32)
+        sq_acc[...] += first.astype(f32) * second.astype(f32)
+
+    proj[...] = jnp.zeros_like(proj)
+    acc[...] = jnp.zeros_like(acc)
+    sq_acc[...] = jnp.zeros_like(sq_acc)
+    multiply(0, v, 0, chunks)
+    send_stats(v)
+    multiply(1, u, 0, chunks // 2)
+    standardize(v)
+    gram_send(d, v)
+    multiply(1, u, chunks // 2, chunks)
+    send_stats(u)
+    standardize(u)
+    gram_send(d, u)
+    diagonal(d)
+    gram_sum(d, v)
+    gram_sum(d, u)
+    gram_use(d)
+
+    def hop(s, carry):
+        before = (0, d - s, d - s >= 0)
+        after = (1, d + s, d + s <= n - 1)
+        for view in (v, u):
+            for side, b, there in (before, after):
+
+                @pl.when(there)
+                def _():
+                    z_copy(b, view, side).wait_recv()
+                    pass_on(b, view, side)
+                    gram_send(b, view)
+
+        for side, b, there in (before, after):
+
+            @pl.when(there)
+            def _():
+                diagonal(b)
+                gram_sum(b, v)
+                gram_sum(b, u)
+
+        for side, b, there in (before, after):
+
+            @pl.when(there)
+            def _():
+                gram_use(b)
+
+        return carry
+
+    lax.fori_loop(1, n, hop, 0)
+
+    diag = jnp.zeros((1, cols), f32)
+    for b in range(n):
+        diag += d_part[b, 0:1]
+    diag = diag / batch
+    diag_loss = jnp.sum((1.0 - diag) ** 2 - redundancy_weight * diag * diag)
+    dg_send[...] = jnp.full(dg_send.shape, diag_loss, f32)
+    for o in range(1, members):
+        remote(dg_send, dg_recv.at[me], g_s.at[0], g_r.at[0], mate(o)[1]).start()
+    pltpu.make_async_copy(dg_send, dg_recv.at[me], g_r.at[0]).start()
+    on_diag = (-2.0 * (1.0 - diag)).astype(bf16).astype(f32) - 2.0 * redundancy_weight * diag
+    sums = jnp.full((8, cols), jnp.sum(sq_acc[...]) / batch, f32)
+    for view in range(2):
+        g = acc[view] * (2.0 * redundancy_weight / batch) + rall[d, 1 - view].astype(f32) * on_diag
+        acc[view] = g
+        sums = jnp.where(row_of == 2 * view, jnp.sum(g, axis=0, keepdims=True), sums)
+        sums = jnp.where(
+            row_of == 2 * view + 1, jnp.sum(g * proj[view], axis=0, keepdims=True), sums
+        )
+    fin_send[...] = sums
+    for o in range(1, n):
+        remote(
+            fin_send, fin_recv.at[d], f_s.at[0], f_r.at[0], {"dp": lax.rem(d + o, n)}
+        ).start()
+    pltpu.make_async_copy(fin_send, fin_recv.at[d], f_r.at[0]).start()
+
+    for c in range(chunks):
+        x_swap(c).wait_send()
+    for view in range(2):
+        drain(stat_recv.at[view, pl.ds(0, n - 1)], st_s.at[view])
+        for b in range(n):
+
+            @pl.when((d < n - 1) & (b <= d))
+            def _():
+                z_copy(b, view, 0).wait_send()
+
+            @pl.when((d > 0) & (b >= d))
+            def _():
+                z_copy(b, view, 1).wait_send()
+
+            drain(k_send.at[b, view, pl.ds(0, members - 1)], a_s.at[b, view])
+            drain(k_full.at[b, view, pl.ds(0, members - 1)], b_s.at[b, view])
+
+    drain(fin_recv, f_r.at[0])
+    drain(fin_recv.at[pl.ds(0, n - 1)], f_s.at[0])
+    total = fin_recv[0]
+    for k in range(1, n):
+        total += fin_recv[k]
+    total = total / batch
+    for view in range(2):
+        out_ref[view] = (
+            inv[view, 0:1]
+            * (
+                acc[view]
+                - total[2 * view : 2 * view + 1]
+                - proj[view] * total[2 * view + 1 : 2 * view + 2]
+            )
+        ).astype(bf16)
+    drain(dg_recv, g_r.at[0])
+    drain(dg_recv.at[pl.ds(0, members - 1)], g_s.at[0])
+    loss = redundancy_weight * total[4:5, 0:128]
+    for k in range(members):
+        loss += dg_recv[k, 0:1]
+    loss_ref[...] = jnp.broadcast_to(loss / (cols * members), (8, 128))
+
+
+def fused(views, weight):
+    n = lax.axis_size("dp")
+    features = lax.axis_size("feature")
+    members = 2 * features
+    rows, width = views.shape[1:]
+    cols = weight.shape[1]
+    part = rows // members
+    return_shapes = (
+        jax.ShapeDtypeStruct((2, rows, cols), bf16),
+        jax.ShapeDtypeStruct((8, 128), f32),
+    )
+    dma = pltpu.SemaphoreType.DMA
+    grad, loss = pl.pallas_call(
+        functools.partial(head_kernel, n, features),
+        out_shape=return_shapes,
+        in_specs=[pl.BlockSpec(memory_space=pl.ANY)] * 2,
+        out_specs=(pl.BlockSpec(memory_space=pltpu.VMEM),) * 2,
+        scratch_shapes=[
+            pltpu.VMEM((width, cols), bf16),
+            pltpu.VMEM((2, rows, width), bf16),
+            pltpu.VMEM((2, rows, cols), f32),
+            pltpu.VMEM((2, rows, cols), f32),
+            pltpu.VMEM((2, 8, cols), f32),
+            pltpu.VMEM((n, 2, rows, cols), bf16),
+            pltpu.VMEM((n, 2, members, part, rows), bf16),
+            pltpu.VMEM((n, 2, members, part, rows), bf16),
+            pltpu.VMEM((n, 2, part, rows), bf16),
+            pltpu.VMEM((n, 2, members, part, rows), bf16),
+            pltpu.VMEM((2, 8, cols), f32),
+            pltpu.VMEM((2, n, 8, cols), f32),
+            pltpu.VMEM((8, cols), f32),
+            pltpu.VMEM((n, 8, cols), f32),
+            pltpu.VMEM((8, 128), f32),
+            pltpu.VMEM((members, 8, 128), f32),
+            pltpu.VMEM((n, 8, cols), f32),
+            pltpu.VMEM((rows, rows), f32),
+            dma((chunks,)),
+            dma((chunks,)),
+            dma((chunks,)),
+            dma((chunks,)),
+            dma((2,)),
+            dma((2,)),
+            dma((2, n, 2)),
+            dma((n, 2)),
+            dma((n, 2)),
+            dma((n, 2)),
+            dma((n, 2)),
+            dma((n, 2)),
+            dma((1,)),
+            dma((1,)),
+            dma((1,)),
+            dma((1,)),
+        ],
+        compiler_params=pltpu.CompilerParams(
+            collective_id=0, has_side_effects=True, vmem_limit_bytes=vmem_bytes
+        ),
+    )(views, weight)
+    return (grad, loss[0, 0])
+
+
+def local(views, weight):
+    n = lax.axis_size("dp")
+    members = lax.axis_size("feature") * lax.axis_size("view")
+    rows, width = views.shape[1:]
+    cols = weight.shape[1]
+    fits = (
+        2 * (width * cols + 2 * rows * width + 8 * rows * cols)
+        + 4 * n * rows * (cols + 4 * rows)
+        < 32 * 1024 * 1024
+    )
+    even = rows % (16 * members) == 0 and rows % 128 == 0 and cols % 128 == 0
+    even = even and width % (128 * chunks) == 0
+    if lax.axis_size("view") == 2 and n > 1 and fits and even:
+        return fused(views, weight)
+    return plain(views, weight)
+
+
 def solution(mesh):
     placed = (P("view", "dp", None), P(None, ("feature", "view")))
     return jax.shard_map(
-        plain,
+        local,
         mesh=mesh,
         in_specs=placed,
         out_specs=(P(None, "dp", ("feature", "view")), P()),

time: 213 us -> 75.3 us (0.35)
  waiting for transfers between devices: 101 us -> 0 us
  Pallas kernels: 0 us -> 71.4 us
  blocking collectives: 64.6 us -> 0 us
  matrix products: 18.5 us -> 0 us
  between operations: 17.2 us -> 0.64 us
  other arithmetic: 6.62 us -> 0 us
    pallas_call x0 -> x1, Pallas kernels: none -> 71.4 us  [fused(): pl.pallas_call(functools.partial(head_kernel, n, features), out_shape=ret...]
    psum x1 -> x0, waiting for transfers between devices: 53.9 us -> none  [plain(): gram = lax.psum(gram.astype(jnp.bfloat16), ('feature', 'view'))]
    psum x2 -> x0, blocking collectives: 49.9 us -> none  [the longest x1 39.1 us: plain(): lax.psum(redundancy_weight * squares_part / members + diag_part / shards,...]
    all_gather x1 -> x0, waiting for transfers between devices: 47.1 us -> none  [plain(): all_rows = lax.all_gather(rounded, 'dp', axis=1, tiled=True)]
    dot_general x4 -> x0, matrix products: 18.5 us -> none  [the longest x1 7.11 us: plain(): own = jnp.dot(views[0], weight, preferred_element_type=jnp.float32)]
    all_gather x1 -> x0, blocking collectives: 14.7 us -> none  [plain(): lax.all_gather(jnp.concatenate([local_mean, local_sq], axis=1), 'dp')]
    rev x2 -> x0, local copies, waits for them, and re-layouts: 4.15 us -> none  [the longest x1 2.28 us: plain(): gram[::-1]]
    reduce_sum x7 -> x0, other arithmetic: 3.35 us -> none  [the longest x1 2.1 us: plain(): jnp.sum(gram[0].astype(jnp.float32) * gram[1].astype(jnp.float32))]
  transfers between devices with their start and end apart: 3 -> 0, of which waited for: 2 -> 0; matrix products, arithmetic and copies ran while one was open for 4% -> 0% of each run, Pallas kernels for 0% -> 0%
where the time goes in v2:
time: 75.3 us; the launch traced here: 75.1 us
  Pallas kernels  71.4 us (95%)
  local copies, waits for them, and re-layouts  3.05 us (4%)
    pallas_call x1, Pallas kernels, fused(): pl.pallas_call(functools.partial(head_kernel, n, features), out_shape=ret...  71.4 us
    unnamed x1, local copies, waits for them, and re-layouts  1.87 us

profile of v2, /device:TPU:0, one launch (start us, length us, event | category | flops | bytes accessed | tf_op | source)
XLA Modules:
  0.0 75.1 jit_solution(14703976886291045810)
XLA Ops:
  0.6 71.4 %shard_map.41 = (bf16[2,256,512]{2,1,0:T(8,128)(2,1)}, f32[8,128]{1,0:T(8,128)}) custom-call(bf16[1,256,8192]{2,1,0:T(8,128)(2,1)} %views_ref.1, bf16[8192,512]{1,0:T(8,128)(2,1)} %w_ref.1), custom_call_target="tpu_custom_call" | custom-call | tf_op jit(solution)/shard_map/pallas_call | solution.py:434
  72.1 1.2 %slice.3 = f32[1,1]{1,0:T(1,128)} slice(f32[8,128]{1,0:T(8,128)} %get-tuple-element.5), slice={[0:1], [0:1]} | slice | bytes 8 | tf_op jit(solution)/shard_map/slice | solution.py:479
  73.3 1.9 %copy.5 = bf16[2,256,512]{2,1,0:T(8,128)(2,1)} copy(bf16[2,256,512]{2,1,0:T(8,128)(2,1)} %get-tuple-element.8) | data formatting | bytes 1048576

commit v3 on v2

--- a/solution.py
+++ b/solution.py
@@ -104,6 +104,9 @@
     k_recv,
     k_red,
     k_full,
+    h_send,
+    h_recv,
+    h_red,
     stat_send,
     stat_recv,
     fin_send,
@@ -124,6 +127,10 @@
     a_r,
     b_s,
     b_r,
+    h_as,
+    h_ar,
+    h_s,
+    h_r,
     f_s,
     f_r,
     g_s,
@@ -260,30 +267,22 @@
         pass_on(d, view, 0)
         pass_on(d, view, 1)
 
-    def gram_send(b, view):
-        g = lax.dot_general(
-            rall[d, view], rall[b, view], (((1,), (1,)), ((), ())), preferred_element_type=f32
-        )
-        k_send[b, view] = g.astype(bf16).reshape(members, part, rows)
+    def spread_gram(left, right, send, recv, ssem, rsem):
+        g = lax.dot_general(left, right, (((1,), (1,)), ((), ())), preferred_element_type=f32)
+        send[...] = g.astype(bf16).reshape(members, part, rows)
         for o in range(1, members):
             t, where = mate(o)
-            remote(
-                k_send.at[b, view, t],
-                k_recv.at[b, view, me],
-                a_s.at[b, view],
-                a_r.at[b, view],
-                where,
-            ).start()
-        pltpu.make_async_copy(
-            k_send.at[b, view, me], k_recv.at[b, view, me], a_r.at[b, view]
-        ).start()
-
-    def gram_sum(b, view):
-        drain(k_recv.at[b, view], a_r.at[b, view])
-        total = k_recv[b, view, 0].astype(f32)
+            remote(send.at[t], recv.at[me], ssem, rsem, where).start()
+        pltpu.make_async_copy(send.at[me], recv.at[me], rsem).start()
+
+    def add_up(recv, rsem):
+        drain(recv, rsem)
+        total = recv[0].astype(f32)
         for k in range(1, members):
-            total += k_recv[b, view, k].astype(f32)
-        k_red[b, view] = total.astype(bf16)
+            total += recv[k].astype(f32)
+        return total.astype(bf16)
+
+    def share_sum(b, view):
         for o in range(1, members):
             remote(
                 k_red.at[b, view],
@@ -294,6 +293,47 @@
             ).start()
         pltpu.make_async_copy(k_red.at[b, view], k_full.at[b, view, me], b_r.at[b, view]).start()
 
+    def gram_send(b, view):
+        spread_gram(
+            rall[d, view],
+            rall[b, view],
+            k_send.at[b, view],
+            k_recv.at[b, view],
+            a_s.at[b, view],
+            a_r.at[b, view],
+        )
+
+    def gram_sum(b, view):
+        k_red[b, view] = add_up(k_recv.at[b, view], a_r.at[b, view])
+        share_sum(b, view)
+
+    helps = (d == 1) | (d == n - 2)
+    end = jnp.where(d == 1, 0, n - 1)
+    far = n - 1 - end
+
+    def help_copy(view):
+        return remote(
+            h_red.at[view], k_red.at[far, view], h_s.at[view], h_r.at[view], {"dp": end}
+        )
+
+    def help_send(view):
+        spread_gram(
+            rall[end, view],
+            rall[far, view],
+            h_send.at[view],
+            h_recv.at[view],
+            h_as.at[view],
+            h_ar.at[view],
+        )
+
+    def help_sum(view):
+        h_red[view] = add_up(h_recv.at[view], h_ar.at[view])
+        help_copy(view).start()
+
+    def relay(b, view):
+        drain(k_red.at[b, view], h_r.at[view])
+        share_sum(b, view)
+
     def diagonal(b):
         cross = rall[b, 0].astype(f32) * rall[b, 1].astype(f32)
         d_part[b] = jnp.broadcast_to(jnp.sum(cross, axis=0, keepdims=True), (8, cols))
@@ -314,45 +354,81 @@
     send_stats(v)
     multiply(1, u, 0, chunks // 2)
     standardize(v)
-    gram_send(d, v)
     multiply(1, u, chunks // 2, chunks)
     send_stats(u)
+    gram_send(d, v)
     standardize(u)
     gram_send(d, u)
     diagonal(d)
     gram_sum(d, v)
-    gram_sum(d, u)
-    gram_use(d)
 
     def hop(s, carry):
-        before = (0, d - s, d - s >= 0)
-        after = (1, d + s, d + s <= n - 1)
-        for view in (v, u):
-            for side, b, there in (before, after):
+        sides = ((0, d - s, d - s >= 0), (1, d + s, d + s <= n - 1))
+        earlier = ((d - s + 1, d - s + 1 >= 0), (d + s - 1, (d + s <= n) & (s > 1)))
+
+        def arrive(view):
+            for side, b, there in sides:
 
                 @pl.when(there)
                 def _():
                     z_copy(b, view, side).wait_recv()
                     pass_on(b, view, side)
-                    gram_send(b, view)
-
-        for side, b, there in (before, after):
+
+                    @pl.when(s < n - 1)
+                    def _():
+                        gram_send(b, view)
+
+            @pl.when(helps & (s == n - 2))
+            def _():
+                help_send(view)
+
+        arrive(v)
+        for b, there in earlier:
 
             @pl.when(there)
             def _():
+                gram_sum(b, u)
+
+        @pl.when(helps & (s == n - 1))
+        def _():
+            help_sum(u)
+
+        for side, b, there in sides:
+
+            @pl.when(there & (s == n - 1))
+            def _():
+                relay(b, v)
+                relay(b, u)
+
+        for b, there in earlier:
+
+            @pl.when(there)
+            def _():
+                gram_use(b)
+
+        arrive(u)
+        for side, b, there in sides:
+
+            @pl.when(there)
+            def _():
+                @pl.when(s < n - 1)
+                def _():
+                    gram_sum(b, v)
+
                 diagonal(b)
-                gram_sum(b, v)
-                gram_sum(b, u)
-
-        for side, b, there in (before, after):
-
-            @pl.when(there)
-            def _():
-                gram_use(b)
+
+        @pl.when(helps & (s == n - 2))
+        def _():
+            help_sum(v)
 
         return carry
 
     lax.fori_loop(1, n, hop, 0)
+    for b in (0, n - 1):
+
+        @pl.when(d == n - 1 - b)
+        def _():
+            gram_use(b)
 
     diag = jnp.zeros((1, cols), f32)
     for b in range(n):
@@ -383,6 +459,12 @@
         x_swap(c).wait_send()
     for view in range(2):
         drain(stat_recv.at[view, pl.ds(0, n - 1)], st_s.at[view])
+
+        @pl.when(helps)
+        def _():
+            drain(h_send.at[view, pl.ds(0, members - 1)], h_as.at[view])
+            help_copy(view).wait_send()
+
         for b in range(n):
 
             @pl.when((d < n - 1) & (b <= d))
@@ -393,7 +475,10 @@
             def _():
                 z_copy(b, view, 1).wait_send()
 
-            drain(k_send.at[b, view, pl.ds(0, members - 1)], a_s.at[b, view])
+            @pl.when((b - d < n - 1) & (d - b < n - 1))
+            def _():
+                drain(k_send.at[b, view, pl.ds(0, members - 1)], a_s.at[b, view])
+
             drain(k_full.at[b, view, pl.ds(0, members - 1)], b_s.at[b, view])
 
     drain(fin_recv, f_r.at[0])
@@ -447,6 +532,9 @@
             pltpu.VMEM((n, 2, members, part, rows), bf16),
             pltpu.VMEM((n, 2, part, rows), bf16),
             pltpu.VMEM((n, 2, members, part, rows), bf16),
+            pltpu.VMEM((2, members, part, rows), bf16),
+            pltpu.VMEM((2, members, part, rows), bf16),
+            pltpu.VMEM((2, part, rows), bf16),
             pltpu.VMEM((2, 8, cols), f32),
             pltpu.VMEM((2, n, 8, cols), f32),
             pltpu.VMEM((8, cols), f32),
@@ -467,6 +555,10 @@
             dma((n, 2)),
             dma((n, 2)),
             dma((n, 2)),
+            dma((2,)),
+            dma((2,)),
+            dma((2,)),
+            dma((2,)),
             dma((1,)),
             dma((1,)),
             dma((1,)),
@@ -491,7 +583,7 @@
     )
     even = rows % (16 * members) == 0 and rows % 128 == 0 and cols % 128 == 0
     even = even and width % (128 * chunks) == 0
-    if lax.axis_size("view") == 2 and n > 1 and fits and even:
+    if lax.axis_size("view") == 2 and n > 3 and fits and even:
         return fused(views, weight)
     return plain(views, weight)
 

time: 75.3 us -> 68.4 us (0.908)
  Pallas kernels: 71.4 us -> 64.6 us
    pallas_call x1, Pallas kernels: 71.4 us -> 64.6 us  [fused(): pl.pallas_call(functools.partial(head_kernel, n, features), out_shape=ret...]
where the time goes in v3:
time: 68.4 us; the launch traced here: 68.2 us
  Pallas kernels  64.6 us (94%)
  local copies, waits for them, and re-layouts  3.05 us (4%)
    pallas_call x1, Pallas kernels, fused(): pl.pallas_call(functools.partial(head_kernel, n, features), out_shape=ret...  64.6 us
    unnamed x1, local copies, waits for them, and re-layouts  1.87 us

profile of v3, /device:TPU:0, one launch (start us, length us, event | category | flops | bytes accessed | tf_op | source)
XLA Modules:
  0.0 68.2 jit_solution(2043720891842728874)
XLA Ops:
  0.6 64.6 %shard_map.41 = (bf16[2,256,512]{2,1,0:T(8,128)(2,1)}, f32[8,128]{1,0:T(8,128)}) custom-call(bf16[1,256,8192]{2,1,0:T(8,128)(2,1)} %views_ref.1, bf16[8192,512]{1,0:T(8,128)(2,1)} %w_ref.1), custom_call_target="tpu_custom_call" | custom-call | tf_op jit(solution)/shard_map/pallas_call | solution.py:519
  65.2 1.2 %slice.3 = f32[1,1]{1,0:T(1,128)} slice(f32[8,128]{1,0:T(8,128)} %get-tuple-element.5), slice={[0:1], [0:1]} | slice | bytes 8 | tf_op jit(solution)/shard_map/slice | solution.py:571
  66.4 1.9 %copy.5 = bf16[2,256,512]{2,1,0:T(8,128)(2,1)} copy(bf16[2,256,512]{2,1,0:T(8,128)(2,1)} %get-tuple-element.8) | data formatting | bytes 1048576

commit v4 on v3

--- a/solution.py
+++ b/solution.py
@@ -360,7 +360,6 @@
     standardize(u)
     gram_send(d, u)
     diagonal(d)
-    gram_sum(d, v)
 
     def hop(s, carry):
         sides = ((0, d - s, d - s >= 0), (1, d + s, d + s <= n - 1))
@@ -374,25 +373,32 @@
                     z_copy(b, view, side).wait_recv()
                     pass_on(b, view, side)
 
-                    @pl.when(s < n - 1)
-                    def _():
-                        gram_send(b, view)
+            for _, b, there in sides:
+
+                @pl.when(there & (s < n - 1))
+                def _():
+                    gram_send(b, view)
 
             @pl.when(helps & (s == n - 2))
             def _():
                 help_send(view)
 
         arrive(v)
-        for b, there in earlier:
-
-            @pl.when(there)
-            def _():
-                gram_sum(b, u)
+
+        @pl.when(s == 1)
+        def _():
+            gram_sum(d, v)
 
         @pl.when(helps & (s == n - 1))
         def _():
             help_sum(u)
 
+        for b, there in earlier:
+
+            @pl.when(there)
+            def _():
+                gram_sum(b, u)
+
         for side, b, there in sides:
 
             @pl.when(there & (s == n - 1))
@@ -402,7 +408,7 @@
 
         for b, there in earlier:
 
-            @pl.when(there)
+            @pl.when(there & (s == n - 1))
             def _():
                 gram_use(b)
 
@@ -420,6 +426,12 @@
         @pl.when(helps & (s == n - 2))
         def _():
             help_sum(v)
+
+        for b, there in earlier:
+
+            @pl.when(there & (s < n - 1))
+            def _():
+                gram_use(b)
 
         return carry
 

time: 68.4 us -> 64.3 us (0.940)
  Pallas kernels: 64.6 us -> 60.4 us
    pallas_call x1, Pallas kernels: 64.6 us -> 60.4 us  [fused(): pl.pallas_call(functools.partial(head_kernel, n, features), out_shape=ret...]
where the time goes in v4:
time: 64.3 us; the launch traced here: 64.1 us
  Pallas kernels  60.4 us (94%)
  local copies, waits for them, and re-layouts  3.05 us (5%)
    pallas_call x1, Pallas kernels, fused(): pl.pallas_call(functools.partial(head_kernel, n, features), out_shape=ret...  60.4 us
    unnamed x1, local copies, waits for them, and re-layouts  1.87 us

profile of v4, /device:TPU:0, one launch (start us, length us, event | category | flops | bytes accessed | tf_op | source)
XLA Modules:
  0.0 64.1 jit_solution(10725963089361245008)
XLA Ops:
  0.6 60.4 %shard_map.41 = (bf16[2,256,512]{2,1,0:T(8,128)(2,1)}, f32[8,128]{1,0:T(8,128)}) custom-call(bf16[1,256,8192]{2,1,0:T(8,128)(2,1)} %views_ref.1, bf16[8192,512]{1,0:T(8,128)(2,1)} %w_ref.1), custom_call_target="tpu_custom_call" | custom-call | tf_op jit(solution)/shard_map/pallas_call | solution.py:531
  61.1 1.2 %slice.3 = f32[1,1]{1,0:T(1,128)} slice(f32[8,128]{1,0:T(8,128)} %get-tuple-element.5), slice={[0:1], [0:1]} | slice | bytes 8 | tf_op jit(solution)/shard_map/slice | solution.py:583
  62.2 1.9 %copy.5 = bf16[2,256,512]{2,1,0:T(8,128)(2,1)} copy(bf16[2,256,512]{2,1,0:T(8,128)(2,1)} %get-tuple-element.8) | data formatting | bytes 1048576

commit v5 on v4

--- a/solution.py
+++ b/solution.py
@@ -347,6 +347,19 @@
         acc[1] += jnp.dot(first, rall[b, 1], preferred_element_type=f32)
         sq_acc[...] += first.astype(f32) * second.astype(f32)
 
+    def gram_use_part(b, view):
+        acc[view] += jnp.dot(
+            k_full[b, 1 - view].reshape(rows, rows), rall[b, view], preferred_element_type=f32
+        )
+
+    def gram_use_early(b):
+        for view in range(2):
+            drain(k_full.at[b, view], b_r.at[b, view])
+        gram_use_part(b, v)
+        sq_acc[...] += k_full[b, 0].reshape(rows, rows).astype(f32) * k_full[b, 1].reshape(
+            rows, rows
+        ).astype(f32)
+
     proj[...] = jnp.zeros_like(proj)
     acc[...] = jnp.zeros_like(acc)
     sq_acc[...] = jnp.zeros_like(sq_acc)
@@ -412,6 +425,12 @@
             def _():
                 gram_use(b)
 
+        for _, b, there in sides:
+
+            @pl.when(there & (s == n - 1))
+            def _():
+                gram_use_early(b)
+
         arrive(u)
         for side, b, there in sides:
 
@@ -440,7 +459,7 @@
 
         @pl.when(d == n - 1 - b)
         def _():
-            gram_use(b)
+            gram_use_part(b, u)
 
     diag = jnp.zeros((1, cols), f32)
     for b in range(n):

time: 64.3 us -> 64.6 us (level)
  no operation moved by 1% of the time
where the time goes in v5:
time: 64.6 us; the launch traced here: 64.4 us
  Pallas kernels  60.7 us (94%)
  local copies, waits for them, and re-layouts  3.05 us (5%)
    pallas_call x1, Pallas kernels, fused(): pl.pallas_call(functools.partial(head_kernel, n, features), out_shape=ret...  60.7 us
    unnamed x1, local copies, waits for them, and re-layouts  1.87 us

profile of v5, /device:TPU:0, one launch (start us, length us, event | category | flops | bytes accessed | tf_op | source)
XLA Modules:
  0.0 64.4 jit_solution(1225684143351563877)
XLA Ops:
  0.6 60.7 %shard_map.41 = (bf16[2,256,512]{2,1,0:T(8,128)(2,1)}, f32[8,128]{1,0:T(8,128)}) custom-call(bf16[1,256,8192]{2,1,0:T(8,128)(2,1)} %views_ref.1, bf16[8192,512]{1,0:T(8,128)(2,1)} %w_ref.1), custom_call_target="tpu_custom_call" | custom-call | tf_op jit(solution)/shard_map/pallas_call | solution.py:550
  61.4 1.2 %slice.3 = f32[1,1]{1,0:T(1,128)} slice(f32[8,128]{1,0:T(8,128)} %get-tuple-element.5), slice={[0:1], [0:1]} | slice | bytes 8 | tf_op jit(solution)/shard_map/slice | solution.py:602
  62.5 1.9 %copy.5 = bf16[2,256,512]{2,1,0:T(8,128)(2,1)} copy(bf16[2,256,512]{2,1,0:T(8,128)(2,1)} %get-tuple-element.8) | data formatting | bytes 1048576
